TPU v7x, 32 devices: a whole 2x2x4 slice. The times are simulated.
32 devices in a mesh: parts: 2 (over x), head: 8 (over z, y), req: 2 (over core).
Axes of the slice: x: 2, y: 2, z: 4, core: 2. Of those that a mesh axis runs over, the one named last changes fastest.
Arguments:
- latent_cache: bfloat16 [16, 2048, 576], P(('parts', 'req'), 'head'), parts along dimension 0, may hold values from -8.5 to 8.5
- lengths: int32 [16], P('parts'), parts along dimension 0, may hold values from 170 to 2048, as said below
- slot_request: int32 [16], P('parts'), parts along dimension 0, may hold values from 0 to 7, each once
- queries: bfloat16 [4, 16, 16, 32, 192], P(None, ('parts', 'req'), None, 'head'), parts along dimension 1, may hold values from -64 to 64
- new_latent: bfloat16 [4, 16, 16, 576], P(None, ('parts', 'req')), parts along dimension 1, may hold values from -6 to 6
- key_up: bfloat16 [32, 128, 512], P('head'), may hold values from -0.25 to 0.25
- value_up: bfloat16 [32, 512, 128], P('head'), may hold values from -2 to 2
- output_weight: bfloat16 [32, 128, 7168], P('head'), may hold values from -0.09375 to 0.09375
Outputs:
- attended_out: bfloat16 [64, 16, 7168], P('head', ('parts', 'req')), parts along dimension 1
There are 2 independent parts, one for each index of `parts`. A program takes and returns all parts, laid end to end along the dimension named above; an argument that names none is the same for every part. Nothing has to cross between parts.
Inputs may be any that keep to these rules, and one draw needn't show every extreme that they name: `lengths`: slots at or beyond a request's length are unused; one request has exactly 2048 and one exactly 170. `slot_request`: decode slots g * 4 to (g + 1) * 4 - 1 form decode group g; every request is served by exactly one slot.
All inputs are finite; a program needn't handle non-finite values.
Results may differ from a plain program's by a relative error of at most 0.014.
Values may be sent and summed in bfloat16 or wider, within the bound.
A program may use at most 128 MiB of HBM per device.

v0:
```python
import jax
import jax.numpy as jnp
from jax import lax
from jax.sharding import PartitionSpec as P


def shards(
    latent_cache, lengths, slot_request, queries, new_latent, key_up, value_up, output_weight
):
    slots_here = latent_cache.shape[0]
    span_here = latent_cache.shape[1]
    cache_width = latent_cache.shape[2]
    nope_width = key_up.shape[1]
    latent_size = key_up.shape[2]
    steps_count = queries.shape[0]
    cont_count = queries.shape[2]
    heads_here = queries.shape[3]
    vhead_width = value_up.shape[2]
    query_rows = steps_count * cont_count * heads_here
    score_scale = (nope_width + cache_width - latent_size) ** (-0.5)
    group_index = lax.axis_index("req")
    my_requests = lax.dynamic_slice_in_dim(slot_request, group_index * slots_here, slots_here)
    matches = my_requests[:, None] == jnp.arange(lengths.shape[0], dtype=jnp.int32)[None, :]
    my_lengths = jnp.sum(jnp.where(matches, lengths[None, :], 0), axis=1)
    absorbed = jnp.einsum(
        "tschd,hdk->stchk", queries[..., :nope_width], key_up, preferred_element_type=jnp.float32
    ).astype(jnp.bfloat16)
    rotary = jnp.transpose(queries[..., nope_width:], (1, 0, 2, 3, 4))
    query_grid = jnp.concatenate([absorbed, rotary], axis=-1)
    flat_queries = query_grid.reshape(slots_here, query_rows, cache_width)
    stacked = latent_cache[None]
    group_count = lax.axis_size("req")
    anchor = my_requests // slots_here
    in_source = my_requests % slots_here
    block_rows = lax.all_gather(stacked, ("head", "req"), axis=0, tiled=True)
    blocks = block_rows.shape[0]
    owners = jnp.arange(blocks, dtype=jnp.int32)
    sender = owners % group_count
    stripe = owners // group_count
    selected = jnp.take(block_rows, in_source, axis=1)
    places = stripe[:, None] * span_here + jnp.arange(span_here, dtype=jnp.int32)[None, :]
    usable = (anchor[None, :, None] == sender[:, None, None]) & (
        places[:, None, :] < my_lengths[None, :, None]
    )
    old_max = jnp.full((slots_here, query_rows), -1e30, jnp.float32)
    blocks = selected.shape[0]
    width_here = selected.shape[2]
    scores = (
        jnp.einsum("srd,jsmd->srjm", flat_queries, selected, preferred_element_type=jnp.float32)
        * score_scale
    )
    scores = scores.reshape(slots_here, query_rows, blocks * width_here)
    usable_mask = jnp.transpose(usable, (1, 0, 2)).reshape(slots_here, 1, blocks * width_here)
    scores = jnp.where(usable_mask, scores, -1e30)
    highest = jnp.maximum(old_max, jnp.max(scores, axis=-1))
    weights = jnp.where(usable_mask, jnp.exp(scores - highest[..., None]), 0.0)
    totals = jnp.sum(weights, axis=-1)
    probs = weights.astype(jnp.bfloat16).reshape(slots_here, query_rows, blocks, width_here)
    values = selected[..., :latent_size]
    weighted = jnp.einsum("srjm,jsmk->srk", probs, values, preferred_element_type=jnp.float32)
    carried = (highest, totals, weighted)
    old_max, old_totals, weighted = carried
    grid_shape = (slots_here, steps_count, cont_count, heads_here)
    old_max = old_max.reshape(grid_shape)
    old_totals = old_totals.reshape(grid_shape)
    weighted = weighted.reshape(grid_shape + (latent_size,))
    own_scores = (
        jnp.einsum("stchd,uscd->stchu", query_grid, new_latent, preferred_element_type=jnp.float32)
        * score_scale
    )
    causal = jnp.arange(steps_count)[:, None] >= jnp.arange(steps_count)[None, :]
    own_mask = causal[None, :, None, None, :]
    own_scores = jnp.where(own_mask, own_scores, -1e30)
    highest = jnp.maximum(old_max, jnp.max(own_scores, axis=-1))
    rescale = jnp.exp(old_max - highest)
    own_weights = jnp.where(own_mask, jnp.exp(own_scores - highest[..., None]), 0.0)
    denominator = old_totals * rescale + jnp.sum(own_weights, axis=-1)
    weighted = weighted * rescale[..., None] + jnp.einsum(
        "stchu,usck->stchk",
        own_weights.astype(jnp.bfloat16),
        new_latent[..., :latent_size],
        preferred_element_type=jnp.float32,
    )
    attended = (weighted / denominator[..., None]).astype(jnp.bfloat16)
    head_out = jnp.einsum(
        "stchk,hkd->stchd", attended, value_up, preferred_element_type=jnp.float32
    ).astype(jnp.bfloat16)
    head_rows = head_out.reshape(slots_here, steps_count * cont_count, heads_here, vhead_width)
    selected = head_rows
    return lax.psum_scatter(
        jnp.einsum(
            "srhd,hdo->rso", selected, output_weight, preferred_element_type=jnp.float32
        ).astype(jnp.bfloat16),
        "head",
        scatter_dimension=0,
        tiled=True,
    )


def solution(mesh):
    in_specs = (
        P(("parts", "req"), "head", None),
        P("parts"),
        P("parts"),
        P(None, ("parts", "req"), None, "head", None),
        P(None, ("parts", "req"), None, None),
        P("head", None, None),
        P("head", None, None),
        P("head", None, None),
    )
    out_specs = P("head", ("parts", "req"), None)
    return jax.shard_map(shards, mesh=mesh, in_specs=in_specs, out_specs=out_specs, check_vma=False)
```

profile of v0, /device:TPU:0, one launch (start us, length us, event | category | flops | bytes accessed | tf_op | source)
XLA Modules:
  0.0 361.4 jit_solution(8031673918906879564)
XLA Ops:
  6.5 0.7 all-gather.3.cloned.1.call-update
  7.3 1.1 slice.13
  8.4 1.1 slice.12
  9.5 0.4 fusion.21
  10.1 1.6 copy.120
  11.7 0.7 slice.15
  12.4 7.0 %fusion.24 = f32[4,16,4,4,4]{3,4,2,1,0:T(4,128)S(1)} fusion(bf16[4,4,16,4,576]{4,2,0,1,3:T(8,128)(2,1)S(1)} %pad_maximum_fusion, bf16[4,4,16,576,1]{3,2,1,0,4:T(8,128)(2,1)S(1)} %bitcast.108), kind=kOutput, calls=%fused_computation.34 | convolution fusion | flops 4718592 | bytes 1490944 | tf_op jit(solution)/shard_map/stchd,uscd->stchu/dot_general | solution.py:68
  19.4 0.5 copy.130
  20.2 0.8 bitcast_reduce_fusion
  21.3 89.4 %all-gather.3.cloned.1.call-done = bf16[64,256,576]{1,2,0:T(8,128)(2,1)} async-done(((bf16[4,256,576]{1,2,0:T(8,128)(2,1)}), bf16[64,256,576]{1,2,0:T(8,128)(2,1)}) %all-gather.3.cloned.1.call-update) | async-done | bytes 18874384 | tf_op jit(solution)/shard_map/all_gather | solution.py:35
  110.7 3.2 mini-gather-slice.5
  113.9 11.7 %fusion.40 = (bf16[16,4,256,256]{2,3,1,0:T(8,128)(2,1)}, bf16[16,4,256,256]{2,3,1,0:T(8,128)(2,1)}) fusion(bf16[16,4,256,576]{2,3,1,0:T(8,128)(2,1)} %bitcast.98), kind=kLoop, calls=%fused_computation.78 | loop fusion | bytes 33554432 | tf_op jit(solution)/shard_map/jit(_take)/gather | solution.py:40
  125.6 2.3 gather_fusion
  127.9 3.1 copy.123
  131.0 4.2 %broadcast.182.clone = bf16[4,16,256,256]{3,2,1,0:T(8,128)(2,1)} broadcast(bf16[]{:T(256)} %constant.89), dimensions={} | broadcast | bytes 8388610
  135.3 34.3 %while.3 = (s32[]{:T(128)}, bf16[16,4,256,256]{2,3,1,0:T(8,128)(2,1)}, s32[4,1]{0,1:T(1,128)S(1)}, bf16[4,16,256,256]{3,2,1,0:T(8,128)(2,1)}, s32[]{:T(128)}) while((s32[]{:T(128)}, bf16[16,4,256,256]{2,3,1,0:T(8,128)(2,1)}, s32[4,1]{0,1:T(1,128)S(1)}, bf16[4,16,256,256]{3,2,1,0:T(8,128)(2,1)}, s32[]{:T(128)}) %tuple.52), condition=%wide.while_cond.1, body=%wide.while_body.1.sunk | while | flops 2 | bytes 12583001 | solution.py:40
  135.3 0.5 constant_dynamic-slice_fusion.10
  135.8 3.7 %constant_dynamic-slice_fusion.11 = bf16[16,1,256,256]{2,3,1,0:T(8,128)(2,1)} fusion(bf16[16,4,256,256]{2,3,1,0:T(8,128)(2,1)} %get-tuple-element.144, s32[]{:T(128)} %bitcast.94), kind=kLoop, calls=%fused_computation.6.clone.1 | loop fusion | bytes 4194308 | tf_op jit(solution)/shard_map/jit(_take)/gather
  139.5 2.8 copy.194
  142.4 1.5 bitcast_dynamic-update-slice_fusion.5
  143.8 0.5 constant_dynamic-slice_fusion.10
  144.4 3.7 %constant_dynamic-slice_fusion.11 = bf16[16,1,256,256]{2,3,1,0:T(8,128)(2,1)} fusion(bf16[16,4,256,256]{2,3,1,0:T(8,128)(2,1)} %get-tuple-element.144, s32[]{:T(128)} %bitcast.94), kind=kLoop, calls=%fused_computation.6.clone.1 | loop fusion | bytes 4194308 | tf_op jit(solution)/shard_map/jit(_take)/gather
  148.1 2.8 copy.194
  150.9 1.5 bitcast_dynamic-update-slice_fusion.5
  152.4 0.5 constant_dynamic-slice_fusion.10
  152.9 3.7 %constant_dynamic-slice_fusion.11 = bf16[16,1,256,256]{2,3,1,0:T(8,128)(2,1)} fusion(bf16[16,4,256,256]{2,3,1,0:T(8,128)(2,1)} %get-tuple-element.144, s32[]{:T(128)} %bitcast.94), kind=kLoop, calls=%fused_computation.6.clone.1 | loop fusion | bytes 4194308 | tf_op jit(solution)/shard_map/jit(_take)/gather
  156.6 2.8 copy.194
  159.5 1.5 bitcast_dynamic-update-slice_fusion.5
  161.0 0.5 constant_dynamic-slice_fusion.10
  161.5 3.7 %constant_dynamic-slice_fusion.11 = bf16[16,1,256,256]{2,3,1,0:T(8,128)(2,1)} fusion(bf16[16,4,256,256]{2,3,1,0:T(8,128)(2,1)} %get-tuple-element.144, s32[]{:T(128)} %bitcast.94), kind=kLoop, calls=%fused_computation.6.clone.1 | loop fusion | bytes 4194308 | tf_op jit(solution)/shard_map/jit(_take)/gather
  165.2 2.8 copy.194
  168.1 1.5 bitcast_dynamic-update-slice_fusion.5
  169.5 4.3 %broadcast.182.clone.1 = bf16[4,16,256,256]{3,2,1,0:T(8,128)(2,1)} broadcast(bf16[]{:T(256)} %constant.89), dimensions={} | broadcast | bytes 8388610
  173.8 34.6 %while.2 = (s32[]{:T(128)}, bf16[16,4,256,256]{2,3,1,0:T(8,128)(2,1)}, s32[4,1]{0,1:T(1,128)S(1)}, bf16[4,16,256,256]{3,2,1,0:T(8,128)(2,1)}, s32[]{:T(128)}) while((s32[]{:T(128)}, bf16[16,4,256,256]{2,3,1,0:T(8,128)(2,1)}, s32[4,1]{0,1:T(1,128)S(1)}, bf16[4,16,256,256]{3,2,1,0:T(8,128)(2,1)}, s32[]{:T(128)}) %tuple.53), condition=%wide.while_cond, body=%wide.while_body.sunk | while | flops 2 | bytes 12583001 | solution.py:40
  173.8 0.6 constant_dynamic-slice_fusion.8
  174.4 3.7 %constant_dynamic-slice_fusion.9 = bf16[16,1,256,256]{2,3,1,0:T(8,128)(2,1)} fusion(bf16[16,4,256,256]{2,3,1,0:T(8,128)(2,1)} %get-tuple-element.159, s32[]{:T(128)} %bitcast.92), kind=kLoop, calls=%fused_computation.3.clone.1 | loop fusion | bytes 4194308 | tf_op jit(solution)/shard_map/jit(_take)/gather
  178.1 2.8 copy.193
  181.0 1.5 bitcast_dynamic-update-slice_fusion.4
  182.5 0.6 constant_dynamic-slice_fusion.8
  183.1 3.7 %constant_dynamic-slice_fusion.9 = bf16[16,1,256,256]{2,3,1,0:T(8,128)(2,1)} fusion(bf16[16,4,256,256]{2,3,1,0:T(8,128)(2,1)} %get-tuple-element.159, s32[]{:T(128)} %bitcast.92), kind=kLoop, calls=%fused_computation.3.clone.1 | loop fusion | bytes 4194308 | tf_op jit(solution)/shard_map/jit(_take)/gather
  186.8 2.8 copy.193
  189.7 1.5 bitcast_dynamic-update-slice_fusion.4
  191.1 0.6 constant_dynamic-slice_fusion.8
  191.7 3.7 %constant_dynamic-slice_fusion.9 = bf16[16,1,256,256]{2,3,1,0:T(8,128)(2,1)} fusion(bf16[16,4,256,256]{2,3,1,0:T(8,128)(2,1)} %get-tuple-element.159, s32[]{:T(128)} %bitcast.92), kind=kLoop, calls=%fused_computation.3.clone.1 | loop fusion | bytes 4194308 | tf_op jit(solution)/shard_map/jit(_take)/gather
  195.4 2.8 copy.193
  198.3 1.5 bitcast_dynamic-update-slice_fusion.4
  199.8 0.6 constant_dynamic-slice_fusion.8
  200.4 3.7 %constant_dynamic-slice_fusion.9 = bf16[16,1,256,256]{2,3,1,0:T(8,128)(2,1)} fusion(bf16[16,4,256,256]{2,3,1,0:T(8,128)(2,1)} %get-tuple-element.159, s32[]{:T(128)} %bitcast.92), kind=kLoop, calls=%fused_computation.3.clone.1 | loop fusion | bytes 4194308 | tf_op jit(solution)/shard_map/jit(_take)/gather
  204.1 2.8 copy.193
  206.9 1.4 bitcast_dynamic-update-slice_fusion.4
  208.4 13.4 %maximum_select_fusion = bf16[16,4,256,576]{3,2,0,1:T(8,128)(2,1)S(1)} fusion(bf16[16,4,256,64]{3,2,0,1:T(8,128)(2,1)} %bitcast.99, bf16[16,4,256,256]{3,2,0,1:T(8,128)(2,1)} %bitcast.96, bf16[16,4,256,256]{3,2,0,1:T(8,128)(2,1)} %bitcast.95, pred[4]{0:T(512)(128)(4,1)S(1)} %get-tuple-element.73), kind=kLoop, calls=%fused_computation.7 | loop fusion | flops 66060288 | bytes 37748740 | tf_op jit(solution)/shard_map/jit(_take)/select_n | solution.py:40
  221.8 13.2 %fusion.2 = (f32[4,256]{1,0:T(4,128)S(1)}, f32[4,256,16,256]{1,3,2,0:T(8,128)}) fusion(pred[4,16,256]{2,1,0:T(8,128)(4,1)S(1)} %compare_and_fusion, bf16[16,4,256,576]{3,2,0,1:T(8,128)(2,1)S(1)} %maximum_select_fusion, bf16[4,256,576,1]{2,0,1,3:T(4,128)(2,1)S(1)} %bitcast.102), kind=kOutput, calls=%fused_computation.12 | convolution fusion | flops 4844420096 | bytes 36851712 | tf_op jit(solution)/shard_map/srd,jsmd->srjm/dot_general | solution.py:49
  235.1 14.3 %fusion.16 = f32[4,256,512]{2,1,0:T(8,128)} fusion(bf16[16,4,256,576]{3,2,0,1:T(8,128)(2,1)} %copy-done.2, f32[4,256,16,256]{1,3,2,0:T(8,128)} %get-tuple-element.80, f32[4,256]{1,0:T(4,128)S(1)} %broadcast_maximum_fusion, pred[4,16,256]{2,1,0:T(8,128)(4,1)S(1)} %compare_and_fusion), kind=kOutput, calls=%fused_computation.28 | convolution fusion | flops 4315938816 | bytes 35672064 | tf_op jit(solution)/shard_map/srjm,jsmk->srk/dot_general | solution.py:60
  249.5 1.8 copy-done.3
  251.3 5.1 %fusion.3 = f32[4,256]{1,0:T(4,128)S(1)} fusion(f32[4,256,16,256]{1,3,2,0:T(8,128)S(1)} %copy-done.3, f32[4,256]{1,0:T(4,128)S(1)} %broadcast_maximum_fusion, pred[4,16,256]{2,1,0:T(8,128)(4,1)S(1)} %compare_and_fusion), kind=kLoop, calls=%fused_computation.13 | loop fusion | flops 20970496 | bytes 16801792 | tf_op jit(solution)/shard_map/reduce_sum | solution.py:57
  256.6 0.2 fusion.34
  256.9 0.5 copy.137
  257.3 2.9 copy.127
  260.6 0.5 fusion.30
  261.2 2.5 convolution_convert_fusion.1
  263.7 5.6 %fusion.6 = bf16[4,8,8,7168]{3,2,1,0:T(8,128)(2,1)S(1)} fusion(bf16[4,64,4,128]{3,1,0,2:T(8,128)(2,1)S(1)} %bitcast.107, bf16[4,128,7168]{2,1,0:T(8,128)(2,1)} %param.15), kind=kOutput, calls=%fused_computation.17 | convolution fusion | flops 1880883200 | bytes 11272192 | tf_op jit(solution)/shard_map/srhd,hdo->rso/dot_general | solution.py:91
  269.3 2.1 copy.166
  271.4 81.0 %reduce-scatter.4.cloned.1.call-done = bf16[8,28672]{1,0:T(8,128)(2,1)} async-done(((bf16[64,28672]{1,0:T(8,128)(2,1)}), bf16[8,28672]{1,0:T(8,128)(2,1)}) %reduce-scatter.4.cloned.1.call-update) | async-done | bytes 458768
  352.4 2.1 copy.143
  (51 shorter events, 1.5 us)
Async XLA Ops:
  6.5 3.0 copy-start
  6.5 5.1 %copy-start.8 = (bf16[4,4,16,576]{3,2,1,0:T(8,128)(2,1)S(1)}, bf16[4,4,16,576]{3,2,1,0:T(8,128)(2,1)}, u32[]{:S(2)}) copy-start(bf16[4,4,16,576]{3,2,1,0:T(8,128)(2,1)} %param.12) | copy-start | bytes 884740
  6.5 104.1 %all-gather.3.cloned.1.call-start = ((), (), s32[]{:S(2)}) async-start(), calls=%async_computation.1 | async-start | bytes 20054016 | tf_op jit(solution)/shard_map/all_gather | solution.py:35
  7.3 345.1 %reduce-scatter.4.cloned.1.call-start = ((), (), s32[]{:S(2)}) async-start(), calls=%async_computation.2 | async-start | bytes 4128768
  8.4 11.6 %copy-start.12 = (s32[8]{0:T(128)S(1)}, s32[8]{0:T(128)}, u32[]{:S(2)}) copy-start(s32[8]{0:T(128)} %param.10) | copy-start | bytes 100
  8.4 11.7 %copy-start.14 = (s32[8]{0:T(128)S(1)}, s32[8]{0:T(128)}, u32[]{:S(2)}) copy-start(s32[8]{0:T(128)} %param.9) | copy-start | bytes 100
  19.9 105.7 %copy-start.5 = (f32[4,16,4,4,4]{1,4,3,2,0:T(4,128)}, f32[4,16,4,4,4]{1,4,3,2,0:T(4,128)S(1)}, u32[]{:S(2)}) copy-start(f32[4,16,4,4,4]{1,4,3,2,0:T(4,128)S(1)} %copy.130) | copy-start | bytes 49156
  19.9 1.1 copy-start.10
  208.4 13.4 %copy-start.4 = (bf16[4,4,16,4,576]{4,0,3,2,1:T(4,128)(2,1)S(1)}, bf16[4,4,16,4,576]{4,0,3,2,1:T(4,128)(2,1)}, u32[]{:S(2)}) copy-start(bf16[4,4,16,4,576]{4,0,3,2,1:T(4,128)(2,1)} %copy.120) | copy-start | bytes 3538948
  221.8 13.2 %copy-start.2 = (bf16[16,4,256,576]{3,2,0,1:T(8,128)(2,1)}, bf16[16,4,256,576]{3,2,0,1:T(8,128)(2,1)S(1)}, u32[]{:S(2)}) copy-start(bf16[16,4,256,576]{3,2,0,1:T(8,128)(2,1)S(1)} %maximum_select_fusion) | copy-start | bytes 56623108
  235.1 16.1 %copy-start.3 = (f32[4,256,16,256]{1,3,2,0:T(8,128)S(1)}, f32[4,256,16,256]{1,3,2,0:T(8,128)}, u32[]{:S(2)}) copy-start(f32[4,256,16,256]{1,3,2,0:T(8,128)} %get-tuple-element.80) | copy-start | bytes 50331652
  251.3 5.3 %copy-start.9 = (f32[4,4,16,4]{2,3,1,0:T(4,128)S(1)}, f32[4,4,16,4]{2,3,1,0:T(4,128)}, u32[]{:S(2)}) copy-start(f32[4,4,16,4]{2,3,1,0:T(4,128)} %bitcast_reduce_fusion) | copy-start | bytes 12292
  251.3 5.3 %copy-start.6 = (f32[4,16,4,4,4]{1,4,3,2,0:T(4,128)S(1)}, f32[4,16,4,4,4]{1,4,3,2,0:T(4,128)}, u32[]{:S(2)}) copy-start(f32[4,16,4,4,4]{1,4,3,2,0:T(4,128)} %copy-done.5) | copy-start | bytes 49156
  251.3 5.3 %copy-start.11 = (pred[4,4]{1,0:T(4,128)(4,1)S(1)}, pred[4,4]{1,0:T(4,128)(4,1)}, u32[]{:S(2)}) copy-start(pred[4,4]{1,0:T(4,128)(4,1)} %copy-done.10) | copy-start | bytes 52
  251.3 9.3 %copy-start.7 = (bf16[4,4,16,512]{3,2,1,0:T(8,128)(2,1)S(1)}, bf16[4,4,16,512]{3,2,1,0:T(8,128)(2,1)}, u32[]{:S(2)}) copy-start(bf16[4,4,16,512]{3,2,1,0:T(8,128)(2,1)} %slice.15) | copy-start | bytes 786436
  251.3 9.9 %copy-start.13 = (bf16[4,512,128]{2,1,0:T(8,128)(2,1)S(1)}, bf16[4,512,128]{2,1,0:T(8,128)(2,1)}, u32[]{:S(2)}) copy-start(bf16[4,512,128]{2,1,0:T(8,128)(2,1)} %param.14) | copy-start | bytes 1572868
  263.7 90.9 %copy-start.1 = (bf16[4,128,512]{2,1,0:T(8,128)(2,1)S(1)}, bf16[4,128,512]{2,1,0:T(8,128)(2,1)}, u32[]{:S(2)}) copy-start(bf16[4,128,512]{2,1,0:T(8,128)(2,1)} %param.13) | copy-start | bytes 1572868
Sparse Core Ops, SparseCore 0:
  9.0 101.6 all-gather.2
  271.5 80.8 reduce-scatter.3
where the time goes:
time: 363 us; the launch traced here: 361 us
  waiting for transfers between devices  171 us (47%)
  local copies, waits for them, and re-layouts  113 us (31%)
  matrix products  43.5 us (12%)
  other arithmetic  20.2 us (6%)
  between operations  13.7 us (4%)
    all_gather x1, waiting for transfers between devices, shards(): block_rows = lax.all_gather(stacked, ('head', 'req'), axis=0, tiled=True)  89.4 us
    unnamed x3, waiting for transfers between devices  81.7 us
    gather x32, local copies, waits for them, and re-layouts  68.8 us
    gather x4, local copies, waits for them, and re-layouts, shards(): selected = jnp.take(block_rows, in_source, axis=1)  20.4 us
    dot_general x1, matrix products, shards(): jnp.einsum('srjm,jsmk->srk', probs, values, preferred_element_type=jnp.fl...  14.3 us
    select_n x1, other arithmetic, shards(): selected = jnp.take(block_rows, in_source, axis=1)  13.4 us
    dot_general x1, matrix products, shards(): jnp.einsum('srd,jsmd->srjm', flat_queries, selected, preferred_element_ty...  13.2 us
    unnamed x34, local copies, waits for them, and re-layouts  12.5 us
  transfers between devices with their start and end apart: 2, of which 2 were waited for; matrix products, arithmetic and copies ran while one was open for 4% of the time, Pallas kernels for 0%

commit v1 on v0

v1 whole, which is shorter than its diff:
```python
import functools

import jax
import jax.numpy as jnp
from jax import lax
from jax.experimental import pallas as pl
from jax.experimental.pallas import tpu as pltpu
from jax.sharding import PartitionSpec as P

MESH = pl.DeviceIdType.MESH
F32 = jnp.float32
BF16 = jnp.bfloat16
LOW = -1e30


def dot_nt(a, b):
    return lax.dot_general(a, b, (((1,), (1,)), ((), ())), preferred_element_type=F32)


def attend(state, absorbed, rotary, keys, rope, mask, scale):
    top, total, acc = state
    scores = (dot_nt(absorbed, keys) + dot_nt(rotary, rope)) * scale
    scores = jnp.where(mask, scores, LOW)
    new_top = jnp.maximum(top, jnp.max(scores, axis=1, keepdims=True))
    weights = jnp.where(mask, jnp.exp(scores - new_top), 0.0)
    rescale = jnp.exp(top - new_top)
    total = total * rescale + jnp.sum(weights, axis=1, keepdims=True)
    acc = acc * rescale + jnp.dot(weights.astype(BF16), keys, preferred_element_type=F32)
    return new_top, total, acc


def own_mask(rows, steps, cont, heads):
    row = lax.broadcasted_iota(jnp.int32, (rows, steps * cont), 0) % (steps * cont)
    col = lax.broadcasted_iota(jnp.int32, (rows, steps * cont), 1)
    return (row % cont == col % cont) & (col // cont <= row // cont)


def attention_kernel(
    scale, steps, cont,
    anchor_ref, source_ref, length_ref,
    cache_ref, query_ref, own_ref, up_ref, value_ref, out_ref,
    full_ref, top_ref, total_ref, acc_ref,
):
    slot = pl.program_id(0)
    heads, tokens, nope = query_ref.shape[1], query_ref.shape[2], up_ref.shape[1]
    stripes, span = cache_ref.shape[0], cache_ref.shape[3]
    latent = up_ref.shape[2]
    rows = heads * tokens
    length = length_ref[slot]
    for h in range(heads):
        q = query_ref[0, h]
        full_ref[pl.ds(h * tokens, tokens), :latent] = jnp.dot(
            q[:, :nope], up_ref[h], preferred_element_type=F32
        ).astype(BF16)
        full_ref[pl.ds(h * tokens, tokens), latent:] = q[:, nope:]
    zero = (jnp.full((rows, 1), LOW, F32), jnp.zeros((rows, 1), F32), jnp.zeros((rows, latent), F32))
    own = own_ref[0]
    state = attend(
        zero, full_ref[:, :latent], full_ref[:, latent:], own[:, :latent], own[:, latent:],
        own_mask(rows, steps, cont, heads), scale,
    )
    top_ref[...], total_ref[...], acc_ref[...] = state
    for stripe in range(stripes):
        @pl.when(stripe * span < length)
        def _():
            block = cache_ref[stripe, 0, 0]
            place = stripe * span + lax.broadcasted_iota(jnp.int32, (rows, span), 1)
            state = attend(
                (top_ref[...], total_ref[...], acc_ref[...]),
                full_ref[:, :latent], full_ref[:, latent:], block[:, :latent], block[:, latent:],
                place < length, scale,
            )
            top_ref[...], total_ref[...], acc_ref[...] = state
    attended = (acc_ref[...] / total_ref[...]).astype(BF16)
    width = value_ref.shape[2]
    for h in range(heads):
        out_ref[0, :, h * width:(h + 1) * width] = jnp.dot(
            attended[h * tokens:(h + 1) * tokens], value_ref[h], preferred_element_type=F32
        ).astype(BF16)


def project_kernel(
    chunk, rows_ref, weight_ref, out_ref,
    outbox, inbox, middle, landed, send_a, recv_a, send_b, recv_b,
):
    count = lax.axis_size("head")
    half = count // 2
    me = lax.axis_index("head")
    mine, odd = me // 2, me % 2
    partner = me + 1 - 2 * odd
    size = out_ref.shape[0]
    chunks = weight_ref.shape[1] // chunk
    barrier = pltpu.get_barrier_semaphore()
    pl.semaphore_signal(barrier, inc=1, device_id={"head": partner}, device_id_type=MESH)
    for i in range(1, half):
        peer = lax.rem(mine + i, half) * 2 + odd
        pl.semaphore_signal(barrier, inc=1, device_id={"head": peer}, device_id_type=MESH)
    pl.semaphore_wait(barrier, half)

    firsts = []
    for c in range(chunks):
        cols = slice(c * chunk, (c + 1) * chunk)
        outbox[c] = jnp.dot(
            rows_ref[1 - odd], weight_ref[:, cols], preferred_element_type=F32
        ).astype(BF16)
        copy = pltpu.make_async_remote_copy(
            src_ref=outbox.at[c], dst_ref=inbox.at[c], send_sem=send_a.at[c], recv_sem=recv_a.at[c],
            device_id={"head": partner}, device_id_type=MESH,
        )
        copy.start()
        firsts.append(copy)
    seconds = []
    for c in range(chunks):
        cols = slice(c * chunk, (c + 1) * chunk)
        product = jnp.dot(rows_ref[odd], weight_ref[:, cols], preferred_element_type=F32)
        firsts[c].wait_recv()
        total = (product + inbox[c].astype(F32)).astype(BF16)
        for k in range(half):
            middle[c, k] = total[k * size:(k + 1) * size]
        for i in range(1, half):
            k = lax.rem(mine + i, half)
            copy = pltpu.make_async_remote_copy(
                src_ref=middle.at[c, k], dst_ref=landed.at[c, i],
                send_sem=send_b.at[c, i], recv_sem=recv_b.at[c, i],
                device_id={"head": k * 2 + odd}, device_id_type=MESH,
            )
            copy.start()
            seconds.append(copy)
    for c in range(chunks):
        total = middle[c, mine].astype(F32)
        for i in range(1, half):
            seconds[c * (half - 1) + i - 1].wait_recv()
            total = total + landed[c, i].astype(F32)
        out_ref[:, c * chunk:(c + 1) * chunk] = total.astype(BF16)
    for copy in firsts + seconds:
        copy.wait_send()


def project(head_out, output_weight):
    count = lax.axis_size("head")
    half = count // 2
    slots, tokens, depth = head_out.shape
    width = output_weight.shape[2]
    per = tokens // count
    size = per * slots
    chunk = 1024 if width % 1024 == 0 else width
    chunks = width // chunk
    rows = jnp.transpose(head_out.reshape(slots, half, 2, per, depth), (2, 1, 3, 0, 4))
    rows = rows.reshape(2, half * size, depth)
    vmem = pl.BlockSpec(memory_space=pltpu.VMEM)
    out = pl.pallas_call(
        functools.partial(project_kernel, chunk),
        out_shape=jax.ShapeDtypeStruct((size, width), BF16),
        in_specs=[vmem, vmem],
        out_specs=vmem,
        scratch_shapes=[
            pltpu.VMEM((chunks, half * size, chunk), BF16),
            pltpu.VMEM((chunks, half * size, chunk), BF16),
            pltpu.VMEM((chunks, half, size, chunk), BF16),
            pltpu.VMEM((chunks, half, size, chunk), BF16),
            pltpu.SemaphoreType.DMA((chunks,)),
            pltpu.SemaphoreType.DMA((chunks,)),
            pltpu.SemaphoreType.DMA((chunks, half)),
            pltpu.SemaphoreType.DMA((chunks, half)),
        ],
        compiler_params=pltpu.CompilerParams(
            collective_id=1, has_side_effects=True, vmem_limit_bytes=48 * 1024 * 1024
        ),
        cost_estimate=pl.CostEstimate(
            flops=4 * half * size * depth * width, bytes_accessed=2 * depth * width, transcendentals=0
        ),
    )(rows, output_weight.reshape(depth, width))
    return out.reshape(per, slots, width)


def shards(
    latent_cache, lengths, slot_request, queries, new_latent, key_up, value_up, output_weight
):
    slots, span, cache_width = latent_cache.shape
    nope, latent = key_up.shape[1], key_up.shape[2]
    steps, _, cont, heads, query_width = queries.shape
    vhead = value_up.shape[2]
    tokens = steps * cont
    rows = tokens * heads
    scale = (nope + cache_width - latent) ** (-0.5)
    group = lax.axis_index("req")
    stripes, groups = lax.axis_size("head"), lax.axis_size("req")
    my_requests = lax.dynamic_slice_in_dim(slot_request, group * slots, slots)
    matches = my_requests[:, None] == jnp.arange(lengths.shape[0], dtype=jnp.int32)[None, :]
    my_lengths = jnp.sum(jnp.where(matches, lengths[None, :], 0), axis=1)
    query_rows = jnp.transpose(queries, (1, 3, 0, 2, 4)).reshape(slots, heads, tokens, query_width)
    own_rows = jnp.transpose(new_latent, (1, 0, 2, 3)).reshape(slots, tokens, cache_width)
    gathered = lax.all_gather(latent_cache[None], ("head", "req"), axis=0, tiled=True)
    gathered = gathered.reshape(stripes, groups, slots, span, cache_width)
    head_out = pl.pallas_call(
        functools.partial(attention_kernel, scale, steps, cont),
        out_shape=jax.ShapeDtypeStruct((slots, tokens, heads * vhead), BF16),
        grid_spec=pltpu.PrefetchScalarGridSpec(
            num_scalar_prefetch=3,
            grid=(slots,),
            in_specs=[
                pl.BlockSpec((stripes, 1, 1, span, cache_width), lambda s, a, i, l: (0, a[s], i[s], 0, 0)),
                pl.BlockSpec((1, heads, tokens, query_width), lambda s, a, i, l: (s, 0, 0, 0)),
                pl.BlockSpec((1, tokens, cache_width), lambda s, a, i, l: (s, 0, 0)),
                pl.BlockSpec((heads, nope, latent), lambda s, a, i, l: (0, 0, 0)),
                pl.BlockSpec((heads, latent, vhead), lambda s, a, i, l: (0, 0, 0)),
            ],
            out_specs=pl.BlockSpec((1, tokens, heads * vhead), lambda s, a, i, l: (s, 0, 0)),
            scratch_shapes=[
                pltpu.VMEM((rows, cache_width), BF16),
                pltpu.VMEM((rows, 1), F32),
                pltpu.VMEM((rows, 1), F32),
                pltpu.VMEM((rows, latent), F32),
            ],
        ),
        compiler_params=pltpu.CompilerParams(vmem_limit_bytes=40 * 1024 * 1024),
    )(my_requests // slots, my_requests % slots, my_lengths, gathered, query_rows, own_rows, key_up, value_up)
    return project(head_out, output_weight)


def solution(mesh):
    in_specs = (
        P(("parts", "req"), "head", None),
        P("parts"),
        P("parts"),
        P(None, ("parts", "req"), None, "head", None),
        P(None, ("parts", "req"), None, None),
        P("head", None, None),
        P("head", None, None),
        P("head", None, None),
    )
    out_specs = P("head", ("parts", "req"), None)
    return jax.shard_map(shards, mesh=mesh, in_specs=in_specs, out_specs=out_specs, check_vma=False)
```

time: 363 us -> 220 us (0.61)
  local copies, waits for them, and re-layouts: 113 us -> 30 us
  Pallas kernels: 0 us -> 72.9 us
  waiting for transfers between devices: 171 us -> 100 us
  matrix products: 43.5 us -> 0 us
  other arithmetic: 20.2 us -> 1.59 us
    gather x36 -> x0, local copies, waits for them, and re-layouts: 89.2 us -> none
    unnamed x3 -> x1, waiting for transfers between devices: 81.7 us -> 0.71 us
    pallas_call x0 -> x2, Pallas kernels: none -> 72.9 us  [the longest x1 54.1 us: project(): pl.pallas_call(functools.partial(project_kernel, chunk), out_shape=jax.Sh...]
    dot_general x7 -> x0, matrix products: 43.5 us -> none  [the longest x1 14.3 us: shards(): jnp.einsum('srjm,jsmk->srk', probs, values, preferred_element_type=jnp.fl...]
    all_gather x0 -> x1, local copies, waits for them, and re-layouts: none -> 26.6 us  [shards(): lax.all_gather(latent_cache[None], ('head', 'req'), axis=0, tiled=True)]
    select_n x3 -> x2, other arithmetic: 13.5 us -> 0.75 us  [the longest x1 0.74 us: shards(): my_requests % slots]
    unnamed x34 -> x4, local copies, waits for them, and re-layouts: 12.5 us -> 0.01 us
    all_gather x1, waiting for transfers between devices: 89.4 us -> 99.6 us  [shards(): lax.all_gather(latent_cache[None], ('head', 'req'), axis=0, tiled=True)]
  transfers between devices with their start and end apart: 2 -> 1, of which waited for: 2 -> 1; matrix products, arithmetic and copies ran while one was open for 4% -> 2% of each run, Pallas kernels for 0% -> 0%
where the time goes in v1:
time: 220 us; the launch traced here: 218 us
  waiting for transfers between devices  100 us (45%)
  Pallas kernels  72.9 us (33%)
  local copies, waits for them, and re-layouts  30 us (14%)
  between operations  13.5 us (6%)
    all_gather x1, waiting for transfers between devices, shards(): lax.all_gather(latent_cache[None], ('head', 'req'), axis=0, tiled=True)  99.6 us
    pallas_call x1, Pallas kernels, project(): pl.pallas_call(functools.partial(project_kernel, chunk), out_shape=jax.Sh...  54.1 us
    all_gather x1, local copies, waits for them, and re-layouts, shards(): lax.all_gather(latent_cache[None], ('head', 'req'), axis=0, tiled=True)  26.6 us
    pallas_call x1, Pallas kernels, shards(): pl.pallas_call(functools.partial(attention_kernel, scale, steps, cont), o...  18.8 us
  transfers between devices with their start and end apart: 1, of which 1 were waited for; matrix products, arithmetic and copies ran while one was open for 2% of the time, Pallas kernels for 0%

profile of v1, /device:TPU:0, one launch (start us, length us, event | category | flops | bytes accessed | tf_op | source)
XLA Modules:
  0.0 218.3 jit_solution(10669005739235436791)
XLA Ops:
  6.5 0.0 all-gather.3.cloned.1.call-start
  6.5 0.7 all-gather.3.cloned.1.call-update
  7.3 1.1 copy.18
  8.4 1.0 copy.19
  9.4 0.7 and_select_fusion
  10.1 0.8 select_reduce_fusion.length_ref
  11.0 0.0 copy-start
  11.0 0.0 copy-start.1
  11.0 99.6 %all-gather.3.cloned.1.call-done = bf16[64,256,576]{1,2,0:T(8,128)(2,1)} async-done(((bf16[4,256,576]{1,2,0:T(8,128)(2,1)}), bf16[64,256,576]{1,2,0:T(8,128)(2,1)}) %all-gather.3.cloned.1.call-update) | async-done | bytes 18874384 | tf_op jit(solution)/shard_map/all_gather | solution.py:193
  110.6 26.6 %copy.17 = bf16[64,256,576]{2,1,0:T(8,128)(2,1)} copy(bf16[64,256,576]{1,2,0:T(8,128)(2,1)} %all-gather.3.cloned.1.call-done) | data formatting | bytes 37748736 | tf_op jit(solution)/shard_map/all_gather | solution.py:193
  137.3 0.0 copy-done
  137.3 0.0 copy-done.1
  137.3 18.8 %shard_map.82 = bf16[4,64,512]{2,1,0:T(8,128)(2,1)S(1)} custom-call(s32[4]{0:T(128)S(1)} %and_select_fusion.1.anchor_ref, s32[4]{0:T(128)S(1)} %get-tuple-element.5.source_ref, s32[4]{0:T(128)S(1)} %select_reduce_fusion.length_ref, bf16[8,2,4,256,576]{4,3,2,1,0:T(8,128)(2,1)} %bitcast.13, bf16[4,4,64,192]{3,2,1,0:T(8,128)(2,1)S(1)} %bitcast.10, ...), custom_call_target="tpu_custom_call" | custom-call | tf_op jit(solution)/shard_map/pallas_call | solution.py:195
  156.1 0.2 copy.22
  156.3 0.1 reshape.27.rows_ref
  156.4 54.1 %shard_map.83 = bf16[32,7168]{1,0:T(8,128)(2,1)S(1)} custom-call(bf16[2,128,512]{2,1,0:T(8,128)(2,1)S(1)} %reshape.27.rows_ref, bf16[512,7168]{1,0:T(8,128)(2,1)} %bitcast.14), custom_call_target="tpu_custom_call" | custom-call | flops 1879048192 | bytes 7340032 | tf_op jit(solution)/shard_map/pallas_call | solution.py:151
  210.5 0.9 reshape.29
  (1 shorter events, 0.0 us)
Async XLA Ops:
  6.5 104.1 %all-gather.3.cloned.1.call-start = ((), (), s32[]{:S(2)}) async-start(), calls=%async_computation | async-start | bytes 20054016 | tf_op jit(solution)/shard_map/all_gather | solution.py:193
  11.0 126.3 %copy-start = (bf16[4,128,512]{2,1,0:T(8,128)(2,1)S(1)}, bf16[4,128,512]{2,1,0:T(8,128)(2,1)}, u32[]{:S(2)}) copy-start(bf16[4,128,512]{2,1,0:T(8,128)(2,1)} %up_ref.1) | copy-start | bytes 1572868
  11.0 126.3 %copy-start.1 = (bf16[4,512,128]{2,1,0:T(8,128)(2,1)S(1)}, bf16[4,512,128]{2,1,0:T(8,128)(2,1)}, u32[]{:S(2)}) copy-start(bf16[4,512,128]{2,1,0:T(8,128)(2,1)} %value_ref.1) | copy-start | bytes 1572868
Sparse Core Ops, SparseCore 0:
  9.0 101.6 all-gather.2

commit v2 on v1

--- a/solution.py
+++ b/solution.py
@@ -37,46 +37,228 @@
 
 def attention_kernel(
     scale, steps, cont,
-    anchor_ref, source_ref, length_ref,
-    cache_ref, query_ref, own_ref, up_ref, value_ref, out_ref,
-    full_ref, top_ref, total_ref, acc_ref,
+    request_ref, length_ref, cache_ref, query_ref, rotary_ref, own_ref, up_ref, value_ref, out_ref,
+    both, blocks, full, top_ref, total_ref, acc_ref, kept, kept_top, kept_total,
+    partial, partial_in, stats, stats_in,
+    swap_send, swap_recv, query_send, query_recv, right_send, right_recv, left_send, left_recv,
+    partial_send, partial_recv, stats_send, stats_recv,
 ):
-    slot = pl.program_id(0)
-    heads, tokens, nope = query_ref.shape[1], query_ref.shape[2], up_ref.shape[1]
-    stripes, span = cache_ref.shape[0], cache_ref.shape[3]
-    latent = up_ref.shape[2]
+    slots, heads, tokens, nope = query_ref.shape
+    latent, rope_width = up_ref.shape[2], rotary_ref.shape[2]
+    width = value_ref.shape[2]
+    groups = latent // rope_width
+    span = cache_ref.shape[1] * groups // (groups + 1)
     rows = heads * tokens
-    length = length_ref[slot]
-    for h in range(heads):
-        q = query_ref[0, h]
-        full_ref[pl.ds(h * tokens, tokens), :latent] = jnp.dot(
-            q[:, :nope], up_ref[h], preferred_element_type=F32
-        ).astype(BF16)
-        full_ref[pl.ds(h * tokens, tokens), latent:] = q[:, nope:]
-    zero = (jnp.full((rows, 1), LOW, F32), jnp.zeros((rows, 1), F32), jnp.zeros((rows, latent), F32))
-    own = own_ref[0]
-    state = attend(
-        zero, full_ref[:, :latent], full_ref[:, latent:], own[:, :latent], own[:, latent:],
-        own_mask(rows, steps, cont, heads), scale,
-    )
-    top_ref[...], total_ref[...], acc_ref[...] = state
-    for stripe in range(stripes):
-        @pl.when(stripe * span < length)
+    half = lax.axis_size("head") // 2
+    me = lax.axis_index("head")
+    mine, odd = me // 2, me % 2
+    partner, right, left = me + 1 - 2 * odd, me + 2, me - 2
+    group = lax.axis_index("req")
+    not_first, not_last = mine > 0, mine < half - 1
+
+    barrier = pltpu.get_barrier_semaphore()
+    pl.semaphore_signal(barrier, inc=1, device_id={"req": 1 - group}, device_id_type=MESH)
+    pl.semaphore_signal(barrier, inc=1, device_id={"head": partner}, device_id_type=MESH)
+
+    @pl.when(not_last)
+    def _():
+        pl.semaphore_signal(barrier, inc=1, device_id={"head": right}, device_id_type=MESH)
+
+    @pl.when(not_first)
+    def _():
+        pl.semaphore_signal(barrier, inc=1, device_id={"head": left}, device_id_type=MESH)
+
+    pl.semaphore_wait(barrier, 4 - (mine == 0).astype(jnp.int32) - (mine == half - 1).astype(jnp.int32))
+
+    def swap():
+        return pltpu.make_async_remote_copy(
+            src_ref=cache_ref, dst_ref=both.at[group], send_sem=swap_send, recv_sem=swap_recv,
+            device_id={"req": 1 - group}, device_id_type=MESH,
+        )
+
+    def swap_in():
+        return pltpu.make_async_remote_copy(
+            src_ref=cache_ref, dst_ref=both.at[1 - group], send_sem=swap_send, recv_sem=swap_recv,
+            device_id={"req": 1 - group}, device_id_type=MESH,
+        )
+
+    def to_partner(source, target, send, recv, slot):
+        return pltpu.make_async_remote_copy(
+            src_ref=source, dst_ref=target, send_sem=send.at[slot], recv_sem=recv.at[slot],
+            device_id={"head": partner}, device_id_type=MESH,
+        )
+
+    def send_query(slot):
+        return to_partner(full.at[slot, 0], full.at[slot, 1], query_send, query_recv, slot)
+
+    def send_partial(slot):
+        return to_partner(partial.at[slot], partial_in.at[slot], partial_send, partial_recv, slot)
+
+    def send_stats(slot):
+        return to_partner(stats.at[slot], stats_in.at[slot], stats_send, stats_recv, slot)
+
+    def along(slot, step, block, send, recv, device):
+        return pltpu.make_async_remote_copy(
+            src_ref=blocks.at[slot, block], dst_ref=blocks.at[slot, block],
+            send_sem=send.at[slot, step], recv_sem=recv.at[slot, step],
+            device_id={"head": device}, device_id_type=MESH,
+        )
+
+    def rightward(slot, step, block):
+        return along(slot, step, block, right_send, right_recv, right)
+
+    def leftward(slot, step, block):
+        return along(slot, step, block, left_send, left_recv, left)
+
+    def send_right(slot, step):
+        @pl.when(not_last & (mine - step >= 0))
         def _():
-            block = cache_ref[stripe, 0, 0]
-            place = stripe * span + lax.broadcasted_iota(jnp.int32, (rows, span), 1)
+            rightward(slot, step, mine - step).start()
+
+    def send_left(slot, step):
+        @pl.when(not_first & (mine + step < half))
+        def _():
+            leftward(slot, step, mine + step).start()
+
+    swap().start()
+    both[group] = cache_ref[...]
+
+    @pl.loop(0, slots)
+    def _(slot):
+        for h in range(heads):
+            full[slot, 0, h * tokens:(h + 1) * tokens, :latent] = jnp.dot(
+                query_ref[slot, h], up_ref[h], preferred_element_type=F32
+            ).astype(BF16)
+        full[slot, 0, :, latent:latent + rope_width] = rotary_ref[slot]
+        full[slot, 0, :, latent + rope_width:] = jnp.zeros(
+            (rows, full.shape[3] - latent - rope_width), BF16
+        )
+        send_query(slot).start()
+
+    swap_in().wait_recv()
+
+    @pl.loop(0, slots)
+    def _(slot):
+        request = request_ref[slot]
+        blocks[slot, mine] = both[request // slots, request % slots]
+
+    for slot in range(min(2, slots)):
+        send_right(slot, 0)
+        send_left(slot, 0)
+
+    generated = own_mask(2 * rows, steps, cont, heads)
+    generated = generated & (lax.broadcasted_iota(jnp.int32, generated.shape, 0) < rows)
+
+    def merge(slot):
+        send_partial(slot).wait_recv()
+        send_stats(slot).wait_recv()
+        other_top, other_total = stats_in[slot, :, :1], stats_in[slot, :, 64:65]
+        top = jnp.maximum(kept_top[slot], other_top)
+        here = jnp.exp(kept_top[slot] - top)
+        there = jnp.exp(other_top - top) * other_total
+        total = kept_total[slot] * here + there
+        attended = (kept[slot] * here + partial_in[slot].astype(F32) * there) / total
+        attended = attended.astype(BF16)
+        for h in range(heads):
+            out_ref[slot, :, h * width:(h + 1) * width] = jnp.dot(
+                attended[h * tokens:(h + 1) * tokens], value_ref[h], preferred_element_type=F32
+            ).astype(BF16)
+
+    @pl.loop(0, slots)
+    def _(slot):
+        length = length_ref[slot]
+
+        def absorb(block):
+            keys = blocks[slot, block, :span]
+            packed = blocks[slot, block, span:]
+            rope = jnp.concatenate(
+                [packed[:, g * rope_width:(g + 1) * rope_width] for g in range(groups)], axis=0
+            )
+            stripe = block * 2 + odd
+            place = stripe * span + lax.broadcasted_iota(jnp.int32, (2 * rows, span), 1)
+            query = full[slot].reshape(2 * rows, full.shape[3])
             state = attend(
                 (top_ref[...], total_ref[...], acc_ref[...]),
-                full_ref[:, :latent], full_ref[:, latent:], block[:, :latent], block[:, latent:],
+                query[:, :latent], query[:, latent:latent + rope_width], keys, rope,
                 place < length, scale,
             )
             top_ref[...], total_ref[...], acc_ref[...] = state
-    attended = (acc_ref[...] / total_ref[...]).astype(BF16)
-    width = value_ref.shape[2]
-    for h in range(heads):
-        out_ref[0, :, h * width:(h + 1) * width] = jnp.dot(
-            attended[h * tokens:(h + 1) * tokens], value_ref[h], preferred_element_type=F32
-        ).astype(BF16)
+
+        send_query(slot).wait_recv()
+        query = full[slot].reshape(2 * rows, full.shape[3])
+        own = own_ref[slot]
+        zero = (
+            jnp.full((2 * rows, 1), LOW, F32),
+            jnp.zeros((2 * rows, 1), F32),
+            jnp.zeros((2 * rows, latent), F32),
+        )
+        state = attend(
+            zero, query[:, :latent], query[:, latent:latent + rope_width],
+            own[:, :latent], own[:, latent:], generated, scale,
+        )
+        top_ref[...], total_ref[...], acc_ref[...] = state
+        absorb(mine)
+        for step in range(half - 1):
+            from_left, from_right = mine - 1 - step >= 0, mine + 1 + step < half
+
+            @pl.when(from_left)
+            def _():
+                rightward(slot, step, mine - 1 - step).wait_recv()
+
+            if step + 1 < half - 1:
+                send_right(slot, step + 1)
+
+            @pl.when(from_right)
+            def _():
+                leftward(slot, step, mine + 1 + step).wait_recv()
+
+            if step + 1 < half - 1:
+                send_left(slot, step + 1)
+
+            @pl.when(from_left)
+            def _():
+                absorb(mine - 1 - step)
+
+            @pl.when(from_right)
+            def _():
+                absorb(mine + 1 + step)
+
+        @pl.when(slot + 2 < slots)
+        def _():
+            send_right(slot + 2, 0)
+            send_left(slot + 2, 0)
+
+        total = total_ref[rows:]
+        partial[slot] = (acc_ref[rows:] / jnp.where(total > 0.0, total, 1.0)).astype(BF16)
+        lane = lax.broadcasted_iota(jnp.int32, (rows, 128), 1)
+        stats[slot] = jnp.where(lane < 64, top_ref[rows:], total)
+        send_partial(slot).start()
+        send_stats(slot).start()
+        kept[slot] = acc_ref[:rows]
+        kept_top[slot] = top_ref[:rows]
+        kept_total[slot] = total_ref[:rows]
+
+        @pl.when(slot > 0)
+        def _():
+            merge(slot - 1)
+
+    merge(slots - 1)
+
+    swap().wait_send()
+
+    @pl.loop(0, slots)
+    def _(slot):
+        send_query(slot).wait_send()
+        send_partial(slot).wait_send()
+        send_stats(slot).wait_send()
+        for step in range(half - 1):
+            @pl.when(not_last & (mine - step >= 0))
+            def _():
+                rightward(slot, step, mine - step).wait_send()
+
+            @pl.when(not_first & (mine + step < half))
+            def _():
+                leftward(slot, step, mine + step).wait_send()
 
 
 def project_kernel(
@@ -188,33 +370,51 @@
     my_requests = lax.dynamic_slice_in_dim(slot_request, group * slots, slots)
     matches = my_requests[:, None] == jnp.arange(lengths.shape[0], dtype=jnp.int32)[None, :]
     my_lengths = jnp.sum(jnp.where(matches, lengths[None, :], 0), axis=1)
+    rope = cache_width - latent
+    packs = latent // rope
     query_rows = jnp.transpose(queries, (1, 3, 0, 2, 4)).reshape(slots, heads, tokens, query_width)
+    rotary_rows = query_rows[..., nope:].reshape(slots, rows, rope)
     own_rows = jnp.transpose(new_latent, (1, 0, 2, 3)).reshape(slots, tokens, cache_width)
-    gathered = lax.all_gather(latent_cache[None], ("head", "req"), axis=0, tiled=True)
-    gathered = gathered.reshape(stripes, groups, slots, span, cache_width)
+    packed = latent_cache[..., latent:].reshape(slots, packs, span // packs, rope)
+    packed = jnp.transpose(packed, (0, 2, 1, 3)).reshape(slots, span // packs, latent)
+    cache_rows = jnp.concatenate([latent_cache[..., :latent], packed], axis=1)
+    deep = span + span // packs
+    vmem, smem = pl.BlockSpec(memory_space=pltpu.VMEM), pl.BlockSpec(memory_space=pltpu.SMEM)
+    half = stripes // 2
+    padded = -(-cache_width // 128) * 128
+    dma = pltpu.SemaphoreType.DMA
     head_out = pl.pallas_call(
         functools.partial(attention_kernel, scale, steps, cont),
         out_shape=jax.ShapeDtypeStruct((slots, tokens, heads * vhead), BF16),
-        grid_spec=pltpu.PrefetchScalarGridSpec(
-            num_scalar_prefetch=3,
-            grid=(slots,),
-            in_specs=[
-                pl.BlockSpec((stripes, 1, 1, span, cache_width), lambda s, a, i, l: (0, a[s], i[s], 0, 0)),
-                pl.BlockSpec((1, heads, tokens, query_width), lambda s, a, i, l: (s, 0, 0, 0)),
-                pl.BlockSpec((1, tokens, cache_width), lambda s, a, i, l: (s, 0, 0)),
-                pl.BlockSpec((heads, nope, latent), lambda s, a, i, l: (0, 0, 0)),
-                pl.BlockSpec((heads, latent, vhead), lambda s, a, i, l: (0, 0, 0)),
-            ],
-            out_specs=pl.BlockSpec((1, tokens, heads * vhead), lambda s, a, i, l: (s, 0, 0)),
-            scratch_shapes=[
-                pltpu.VMEM((rows, cache_width), BF16),
-                pltpu.VMEM((rows, 1), F32),
-                pltpu.VMEM((rows, 1), F32),
-                pltpu.VMEM((rows, latent), F32),
-            ],
+        in_specs=[smem, smem] + [vmem] * 6,
+        out_specs=vmem,
+        scratch_shapes=[
+            pltpu.VMEM((groups, slots, deep, latent), BF16),
+            pltpu.VMEM((slots, half, deep, latent), BF16),
+            pltpu.VMEM((slots, 2, rows, padded), BF16),
+            pltpu.VMEM((2 * rows, 1), F32),
+            pltpu.VMEM((2 * rows, 1), F32),
+            pltpu.VMEM((2 * rows, latent), F32),
+            pltpu.VMEM((slots, rows, latent), F32),
+            pltpu.VMEM((slots, rows, 1), F32),
+            pltpu.VMEM((slots, rows, 1), F32),
+            pltpu.VMEM((slots, rows, latent), BF16),
+            pltpu.VMEM((slots, rows, latent), BF16),
+            pltpu.VMEM((slots, rows, 128), F32),
+            pltpu.VMEM((slots, rows, 128), F32),
+            dma, dma, dma((slots,)), dma((slots,)),
+            dma((slots, half - 1)), dma((slots, half - 1)), dma((slots, half - 1)), dma((slots, half - 1)),
+            dma((slots,)), dma((slots,)), dma((slots,)), dma((slots,)),
+        ],
+        compiler_params=pltpu.CompilerParams(
+            collective_id=2, has_side_effects=True, vmem_limit_bytes=48 * 1024 * 1024
         ),
-        compiler_params=pltpu.CompilerParams(vmem_limit_bytes=40 * 1024 * 1024),
-    )(my_requests // slots, my_requests % slots, my_lengths, gathered, query_rows, own_rows, key_up, value_up)
+        cost_estimate=pl.CostEstimate(
+            flops=4 * slots * rows * stripes * span * latent,
+            bytes_accessed=2 * slots * deep * latent,
+            transcendentals=slots * rows * stripes * span,
+        ),
+    )(my_requests, my_lengths, cache_rows, query_rows[..., :nope], rotary_rows, own_rows, key_up, value_up)
     return project(head_out, output_weight)
 
 

time: 220 us -> 161 us (0.73)
  waiting for transfers between devices: 100 us -> 0 us
  Pallas kernels: 72.9 us -> 152 us
  local copies, waits for them, and re-layouts: 30 us -> 7.01 us
  between operations: 13.5 us -> 0.13 us
    all_gather x1 -> x0, waiting for transfers between devices: 99.6 us -> none  [shards(): lax.all_gather(latent_cache[None], ('head', 'req'), axis=0, tiled=True)]
    pallas_call x1, Pallas kernels: 18.8 us -> 100 us  [shards(): pl.pallas_call(functools.partial(attention_kernel, scale, steps, cont), o...]
    all_gather x1 -> x0, local copies, waits for them, and re-layouts: 26.6 us -> none  [shards(): lax.all_gather(latent_cache[None], ('head', 'req'), axis=0, tiled=True)]
    unnamed x4 -> x10, local copies, waits for them, and re-layouts: 0.01 us -> 2.62 us
  transfers between devices with their start and end apart: 1 -> 0, of which waited for: 1 -> 0; matrix products, arithmetic and copies ran while one was open for 2% -> 0% of each run, Pallas kernels for 0% -> 0%
where the time goes in v2:
time: 161 us
  Pallas kernels  152 us (94%)
  local copies, waits for them, and re-layouts  7.01 us (4%)
    pallas_call x1, Pallas kernels, shards(): pl.pallas_call(functools.partial(attention_kernel, scale, steps, cont), o...  100 us
    pallas_call x1, Pallas kernels, project(): pl.pallas_call(functools.partial(project_kernel, chunk), out_shape=jax.Sh...  52.1 us

profile of v2, /device:TPU:0, one launch (start us, length us, event | category | flops | bytes accessed | tf_op | source)
XLA Modules:
  0.0 160.5 jit_solution(17849511473930805203)
XLA Ops:
  0.0 0.7 dynamic_slice.3.request_ref
  0.7 0.8 select_reduce_fusion.length_ref
  1.6 0.9 slice.13
  2.5 0.2 copy.27
  2.7 0.1 copy.22
  2.8 0.0 slice-start
  2.8 0.2 reshape.30
  3.0 1.0 slice-done
  4.0 0.5 copy.26
  4.5 0.0 copy-start.2
  4.6 0.1 pad_maximum_fusion.cache_ref
  4.6 0.0 copy-start.3
  4.7 0.9 copy-done.2
  5.6 0.0 copy-start
  5.6 0.0 copy-start.1
  5.6 0.1 copy.23
  5.8 0.0 copy-done.3
  5.8 0.8 copy-done
  6.7 0.2 copy-done.1
  6.8 100.4 %shard_map.82 = bf16[4,64,512]{2,1,0:T(8,128)(2,1)S(1)} custom-call(s32[4]{0:T(128)S(1)} %dynamic_slice.3.request_ref, s32[4]{0:T(128)S(1)} %select_reduce_fusion.length_ref, bf16[4,288,512]{2,1,0:T(8,128)(2,1)S(1)} %pad_maximum_fusion.cache_ref, bf16[4,4,64,128]{3,2,1,0:T(8,128)(2,1)S(1)} %slice.16.query_ref, bf16[4,256,64]{2,1,0:T(8,128)(2,1)S(1)} %bitcast.16, ...), custom_call_target="tpu_custom_call" | custom-call | flops 4294967296 | bytes 1179648 | tf_op jit(solution)/shard_map/pallas_call | solution.py:386
  107.2 0.2 copy.29
  107.4 0.1 reshape.35.rows_ref
  107.5 52.1 %shard_map.83 = bf16[32,7168]{1,0:T(8,128)(2,1)S(1)} custom-call(bf16[2,128,512]{2,1,0:T(8,128)(2,1)S(1)} %reshape.35.rows_ref, bf16[512,7168]{1,0:T(8,128)(2,1)} %bitcast.18), custom_call_target="tpu_custom_call" | custom-call | flops 1879048192 | bytes 7340032 | tf_op jit(solution)/shard_map/pallas_call | solution.py:333
  159.6 0.9 reshape.37
  (3 shorter events, 0.1 us)
Async XLA Ops:
  2.8 1.2 slice-start
  4.5 1.0 copy-start.2
  4.6 1.2 copy-start.3
  5.6 1.1 copy-start
  5.6 1.2 copy-start.1

commit v3 on v2

--- a/solution.py
+++ b/solution.py
@@ -29,19 +29,23 @@
     return new_top, total, acc
 
 
-def own_mask(rows, steps, cont, heads):
-    row = lax.broadcasted_iota(jnp.int32, (rows, steps * cont), 0) % (steps * cont)
-    col = lax.broadcasted_iota(jnp.int32, (rows, steps * cont), 1)
+def own_mask(rows, steps, cont, per):
+    tokens = steps * cont
+    row = lax.broadcasted_iota(jnp.int32, (rows, tokens), 0) % tokens
+    odd, rest = row // (tokens // 2), row % (tokens // 2)
+    row = (2 * (rest // per) + odd) * per + rest % per
+    col = lax.broadcasted_iota(jnp.int32, (rows, tokens), 1)
     return (row % cont == col % cont) & (col // cont <= row // cont)
 
 
 def attention_kernel(
     scale, steps, cont,
-    request_ref, length_ref, cache_ref, query_ref, rotary_ref, own_ref, up_ref, value_ref, out_ref,
+    request_ref, length_ref, cache_ref, query_ref, rotary_ref, own_ref, up_ref, value_ref, weight_hbm, out_ref,
     both, blocks, full, top_ref, total_ref, acc_ref, kept, kept_top, kept_total,
     partial, partial_in, stats, stats_in,
     swap_send, swap_recv, query_send, query_recv, right_send, right_recv, left_send, left_recv,
     partial_send, partial_recv, stats_send, stats_recv,
+    weight, weight_sem, head_out, outbox, inbox, middle, landed, pair_send, pair_recv, line_send, line_recv,
 ):
     slots, heads, tokens, nope = query_ref.shape
     latent, rope_width = up_ref.shape[2], rotary_ref.shape[2]
@@ -60,15 +64,10 @@
     pl.semaphore_signal(barrier, inc=1, device_id={"req": 1 - group}, device_id_type=MESH)
     pl.semaphore_signal(barrier, inc=1, device_id={"head": partner}, device_id_type=MESH)
 
-    @pl.when(not_last)
-    def _():
-        pl.semaphore_signal(barrier, inc=1, device_id={"head": right}, device_id_type=MESH)
-
-    @pl.when(not_first)
-    def _():
-        pl.semaphore_signal(barrier, inc=1, device_id={"head": left}, device_id_type=MESH)
-
-    pl.semaphore_wait(barrier, 4 - (mine == 0).astype(jnp.int32) - (mine == half - 1).astype(jnp.int32))
+    for i in range(1, half):
+        peer = lax.rem(mine + i, half) * 2 + odd
+        pl.semaphore_signal(barrier, inc=1, device_id={"head": peer}, device_id_type=MESH)
+    pl.semaphore_wait(barrier, half + 1)
 
     def swap():
         return pltpu.make_async_remote_copy(
@@ -120,7 +119,61 @@
         def _():
             leftward(slot, step, mine + step).start()
 
+    def load_weight():
+        return pltpu.make_async_copy(weight_hbm, weight, weight_sem)
+
+    per = tokens // (2 * half)
+    pieces, chunks, chunk = middle.shape[3] // per, middle.shape[1], middle.shape[4]
+
+    def columns(c, piece):
+        start = piece * chunks * chunk + c * chunk
+        return slice(start, start + chunk)
+
+    def send_pair(slot, c):
+        return pltpu.make_async_remote_copy(
+            src_ref=outbox.at[slot, c], dst_ref=inbox.at[slot, c],
+            send_sem=pair_send.at[slot, c], recv_sem=pair_recv.at[slot, c],
+            device_id={"head": partner}, device_id_type=MESH,
+        )
+
+    def send_line(slot, c, i):
+        k = lax.rem(mine + i, half)
+        return pltpu.make_async_remote_copy(
+            src_ref=middle.at[slot, c, k], dst_ref=landed.at[slot, c, i],
+            send_sem=line_send.at[slot, c, i], recv_sem=line_recv.at[slot, c, i],
+            device_id={"head": k * 2 + odd}, device_id_type=MESH,
+        )
+
+    def project_partner(slot):
+        lines = head_out[slot, 1 - odd]
+        for c in range(chunks):
+            for piece in range(pieces):
+                outbox[slot, c, :, piece * chunk:(piece + 1) * chunk] = jnp.dot(
+                    lines, weight[:, columns(c, piece)], preferred_element_type=F32
+                ).astype(BF16)
+            send_pair(slot, c).start()
+
+    def project_mine(slot):
+        lines = head_out[slot, odd]
+        for c in range(chunks):
+            products = [
+                jnp.dot(lines, weight[:, columns(c, piece)], preferred_element_type=F32)
+                for piece in range(pieces)
+            ]
+            send_pair(slot, c).wait_recv()
+            arrived = inbox[slot, c].astype(F32)
+            sums = [
+                products[piece] + arrived[:, piece * chunk:(piece + 1) * chunk] for piece in range(pieces)
+            ]
+            for k in range(half):
+                middle[slot, c, k] = jnp.concatenate(
+                    [part[k * per:(k + 1) * per] for part in sums], axis=0
+                ).astype(BF16)
+            for i in range(1, half):
+                send_line(slot, c, i).start()
+
     swap().start()
+    load_weight().start()
     both[group] = cache_ref[...]
 
     @pl.loop(0, slots)
@@ -139,14 +192,14 @@
 
     @pl.loop(0, slots)
     def _(slot):
-        request = request_ref[slot]
+        request = request_ref[group * slots + slot]
         blocks[slot, mine] = both[request // slots, request % slots]
 
     for slot in range(min(2, slots)):
         send_right(slot, 0)
         send_left(slot, 0)
 
-    generated = own_mask(2 * rows, steps, cont, heads)
+    generated = own_mask(2 * rows, steps, cont, per)
     generated = generated & (lax.broadcasted_iota(jnp.int32, generated.shape, 0) < rows)
 
     def merge(slot):
@@ -160,13 +213,15 @@
         attended = (kept[slot] * here + partial_in[slot].astype(F32) * there) / total
         attended = attended.astype(BF16)
         for h in range(heads):
-            out_ref[slot, :, h * width:(h + 1) * width] = jnp.dot(
+            values = jnp.dot(
                 attended[h * tokens:(h + 1) * tokens], value_ref[h], preferred_element_type=F32
             ).astype(BF16)
+            head_out[slot, 0, :, h * width:(h + 1) * width] = values[:tokens // 2]
+            head_out[slot, 1, :, h * width:(h + 1) * width] = values[tokens // 2:]
 
     @pl.loop(0, slots)
     def _(slot):
-        length = length_ref[slot]
+        length = length_ref[request_ref[group * slots + slot]]
 
         def absorb(block):
             keys = blocks[slot, block, :span]
@@ -198,6 +253,16 @@
         )
         top_ref[...], total_ref[...], acc_ref[...] = state
         absorb(mine)
+
+        @pl.when(slot == 1)
+        def _():
+            load_weight().wait()
+
+        @pl.when(slot > 0)
+        def _():
+            merge(slot - 1)
+            project_partner(slot - 1)
+
         for step in range(half - 1):
             from_left, from_right = mine - 1 - step >= 0, mine + 1 + step < half
 
@@ -240,9 +305,20 @@
 
         @pl.when(slot > 0)
         def _():
-            merge(slot - 1)
+            project_mine(slot - 1)
 
     merge(slots - 1)
+    project_partner(slots - 1)
+    project_mine(slots - 1)
+
+    @pl.loop(0, slots)
+    def _(slot):
+        for c in range(chunks):
+            total = middle[slot, c, mine].astype(F32)
+            for i in range(1, half):
+                send_line(slot, c, i).wait_recv()
+                total = total + landed[slot, c, i].astype(F32)
+            out_ref[slot, :, c * chunk:(c + 1) * chunk] = total.astype(BF16)
 
     swap().wait_send()
 
@@ -251,6 +327,10 @@
         send_query(slot).wait_send()
         send_partial(slot).wait_send()
         send_stats(slot).wait_send()
+        for c in range(chunks):
+            send_pair(slot, c).wait_send()
+            for i in range(1, half):
+                send_line(slot, c, i).wait_send()
         for step in range(half - 1):
             @pl.when(not_last & (mine - step >= 0))
             def _():
@@ -259,100 +339,6 @@
             @pl.when(not_first & (mine + step < half))
             def _():
                 leftward(slot, step, mine + step).wait_send()
-
-
-def project_kernel(
-    chunk, rows_ref, weight_ref, out_ref,
-    outbox, inbox, middle, landed, send_a, recv_a, send_b, recv_b,
-):
-    count = lax.axis_size("head")
-    half = count // 2
-    me = lax.axis_index("head")
-    mine, odd = me // 2, me % 2
-    partner = me + 1 - 2 * odd
-    size = out_ref.shape[0]
-    chunks = weight_ref.shape[1] // chunk
-    barrier = pltpu.get_barrier_semaphore()
-    pl.semaphore_signal(barrier, inc=1, device_id={"head": partner}, device_id_type=MESH)
-    for i in range(1, half):
-        peer = lax.rem(mine + i, half) * 2 + odd
-        pl.semaphore_signal(barrier, inc=1, device_id={"head": peer}, device_id_type=MESH)
-    pl.semaphore_wait(barrier, half)
-
-    firsts = []
-    for c in range(chunks):
-        cols = slice(c * chunk, (c + 1) * chunk)
-        outbox[c] = jnp.dot(
-            rows_ref[1 - odd], weight_ref[:, cols], preferred_element_type=F32
-        ).astype(BF16)
-        copy = pltpu.make_async_remote_copy(
-            src_ref=outbox.at[c], dst_ref=inbox.at[c], send_sem=send_a.at[c], recv_sem=recv_a.at[c],
-            device_id={"head": partner}, device_id_type=MESH,
-        )
-        copy.start()
-        firsts.append(copy)
-    seconds = []
-    for c in range(chunks):
-        cols = slice(c * chunk, (c + 1) * chunk)
-        product = jnp.dot(rows_ref[odd], weight_ref[:, cols], preferred_element_type=F32)
-        firsts[c].wait_recv()
-        total = (product + inbox[c].astype(F32)).astype(BF16)
-        for k in range(half):
-            middle[c, k] = total[k * size:(k + 1) * size]
-        for i in range(1, half):
-            k = lax.rem(mine + i, half)
-            copy = pltpu.make_async_remote_copy(
-                src_ref=middle.at[c, k], dst_ref=landed.at[c, i],
-                send_sem=send_b.at[c, i], recv_sem=recv_b.at[c, i],
-                device_id={"head": k * 2 + odd}, device_id_type=MESH,
-            )
-            copy.start()
-            seconds.append(copy)
-    for c in range(chunks):
-        total = middle[c, mine].astype(F32)
-        for i in range(1, half):
-            seconds[c * (half - 1) + i - 1].wait_recv()
-            total = total + landed[c, i].astype(F32)
-        out_ref[:, c * chunk:(c + 1) * chunk] = total.astype(BF16)
-    for copy in firsts + seconds:
-        copy.wait_send()
-
-
-def project(head_out, output_weight):
-    count = lax.axis_size("head")
-    half = count // 2
-    slots, tokens, depth = head_out.shape
-    width = output_weight.shape[2]
-    per = tokens // count
-    size = per * slots
-    chunk = 1024 if width % 1024 == 0 else width
-    chunks = width // chunk
-    rows = jnp.transpose(head_out.reshape(slots, half, 2, per, depth), (2, 1, 3, 0, 4))
-    rows = rows.reshape(2, half * size, depth)
-    vmem = pl.BlockSpec(memory_space=pltpu.VMEM)
-    out = pl.pallas_call(
-        functools.partial(project_kernel, chunk),
-        out_shape=jax.ShapeDtypeStruct((size, width), BF16),
-        in_specs=[vmem, vmem],
-        out_specs=vmem,
-        scratch_shapes=[
-            pltpu.VMEM((chunks, half * size, chunk), BF16),
-            pltpu.VMEM((chunks, half * size, chunk), BF16),
-            pltpu.VMEM((chunks, half, size, chunk), BF16),
-            pltpu.VMEM((chunks, half, size, chunk), BF16),
-            pltpu.SemaphoreType.DMA((chunks,)),
-            pltpu.SemaphoreType.DMA((chunks,)),
-            pltpu.SemaphoreType.DMA((chunks, half)),
-            pltpu.SemaphoreType.DMA((chunks, half)),
-        ],
-        compiler_params=pltpu.CompilerParams(
-            collective_id=1, has_side_effects=True, vmem_limit_bytes=48 * 1024 * 1024
-        ),
-        cost_estimate=pl.CostEstimate(
-            flops=4 * half * size * depth * width, bytes_accessed=2 * depth * width, transcendentals=0
-        ),
-    )(rows, output_weight.reshape(depth, width))
-    return out.reshape(per, slots, width)
 
 
 def shards(
@@ -365,14 +351,18 @@
     tokens = steps * cont
     rows = tokens * heads
     scale = (nope + cache_width - latent) ** (-0.5)
-    group = lax.axis_index("req")
     stripes, groups = lax.axis_size("head"), lax.axis_size("req")
-    my_requests = lax.dynamic_slice_in_dim(slot_request, group * slots, slots)
-    matches = my_requests[:, None] == jnp.arange(lengths.shape[0], dtype=jnp.int32)[None, :]
-    my_lengths = jnp.sum(jnp.where(matches, lengths[None, :], 0), axis=1)
+    half = stripes // 2
+    per = tokens // stripes
+    pieces = max(1, 16 // per)
+    depth, out_width = heads * vhead, output_weight.shape[2]
+    reach = out_width // pieces
+    chunk = 896 if reach % 896 == 0 else reach
+    chunks = reach // chunk
     rope = cache_width - latent
     packs = latent // rope
-    query_rows = jnp.transpose(queries, (1, 3, 0, 2, 4)).reshape(slots, heads, tokens, query_width)
+    query_rows = jnp.transpose(queries, (1, 3, 0, 2, 4)).reshape(slots, heads, half, 2, per, query_width)
+    query_rows = jnp.transpose(query_rows, (0, 1, 3, 2, 4, 5)).reshape(slots, heads, tokens, query_width)
     rotary_rows = query_rows[..., nope:].reshape(slots, rows, rope)
     own_rows = jnp.transpose(new_latent, (1, 0, 2, 3)).reshape(slots, tokens, cache_width)
     packed = latent_cache[..., latent:].reshape(slots, packs, span // packs, rope)
@@ -380,13 +370,12 @@
     cache_rows = jnp.concatenate([latent_cache[..., :latent], packed], axis=1)
     deep = span + span // packs
     vmem, smem = pl.BlockSpec(memory_space=pltpu.VMEM), pl.BlockSpec(memory_space=pltpu.SMEM)
-    half = stripes // 2
     padded = -(-cache_width // 128) * 128
     dma = pltpu.SemaphoreType.DMA
-    head_out = pl.pallas_call(
+    summed = pl.pallas_call(
         functools.partial(attention_kernel, scale, steps, cont),
-        out_shape=jax.ShapeDtypeStruct((slots, tokens, heads * vhead), BF16),
-        in_specs=[smem, smem] + [vmem] * 6,
+        out_shape=jax.ShapeDtypeStruct((slots, pieces * per, reach), BF16),
+        in_specs=[smem, smem] + [vmem] * 6 + [pl.BlockSpec(memory_space=pl.ANY)],
         out_specs=vmem,
         scratch_shapes=[
             pltpu.VMEM((groups, slots, deep, latent), BF16),
@@ -405,6 +394,15 @@
             dma, dma, dma((slots,)), dma((slots,)),
             dma((slots, half - 1)), dma((slots, half - 1)), dma((slots, half - 1)), dma((slots, half - 1)),
             dma((slots,)), dma((slots,)), dma((slots,)), dma((slots,)),
+            pltpu.VMEM((depth, out_width), BF16),
+            dma,
+            pltpu.VMEM((slots, 2, tokens // 2, depth), BF16),
+            pltpu.VMEM((slots, chunks, half * per, pieces * chunk), BF16),
+            pltpu.VMEM((slots, chunks, half * per, pieces * chunk), BF16),
+            pltpu.VMEM((slots, chunks, half, pieces * per, chunk), BF16),
+            pltpu.VMEM((slots, chunks, half, pieces * per, chunk), BF16),
+            dma((slots, chunks)), dma((slots, chunks)),
+            dma((slots, chunks, half)), dma((slots, chunks, half)),
         ],
         compiler_params=pltpu.CompilerParams(
             collective_id=2, has_side_effects=True, vmem_limit_bytes=48 * 1024 * 1024
@@ -414,8 +412,10 @@
             bytes_accessed=2 * slots * deep * latent,
             transcendentals=slots * rows * stripes * span,
         ),
-    )(my_requests, my_lengths, cache_rows, query_rows[..., :nope], rotary_rows, own_rows, key_up, value_up)
-    return project(head_out, output_weight)
+    )(slot_request, lengths, cache_rows, query_rows[..., :nope], rotary_rows, own_rows, key_up, value_up,
+      output_weight.reshape(depth, out_width))
+    summed = jnp.transpose(summed.reshape(slots, pieces, per, reach), (2, 0, 1, 3))
+    return summed.reshape(per, slots, out_width)
 
 
 def solution(mesh):

time: 161 us -> 145 us (0.901)
  Pallas kernels: 152 us -> 138 us
    pallas_call x1 -> x0, Pallas kernels: 52.1 us -> none  [project(): pl.pallas_call(functools.partial(project_kernel, chunk), out_shape=jax.Sh...]
    pallas_call x1, Pallas kernels: 100 us -> 138 us  [shards(): pl.pallas_call(functools.partial(attention_kernel, scale, steps, cont), o...]
where the time goes in v3:
time: 145 us
  Pallas kernels  138 us (95%)
  local copies, waits for them, and re-layouts  6.48 us (4%)
    pallas_call x1, Pallas kernels, shards(): pl.pallas_call(functools.partial(attention_kernel, scale, steps, cont), o...  138 us

profile of v3, /device:TPU:0, one launch (start us, length us, event | category | flops | bytes accessed | tf_op | source)
XLA Modules:
  0.0 145.1 jit_solution(7341266325028516338)
XLA Ops:
  0.0 0.9 slice.13
  0.9 0.2 copy.21
  1.1 0.1 copy.16
  1.2 0.0 slice-start
  1.2 0.2 reshape.28
  1.4 1.0 slice-done
  2.4 0.5 copy.20
  3.0 0.0 copy-start.4
  3.0 0.1 pad_maximum_fusion.cache_ref
  3.1 0.0 copy-start.5
  3.1 0.9 copy-done.4
  4.0 0.0 copy-start
  4.0 0.0 copy-start.1
  4.0 0.0 copy-start.2
  4.0 0.0 copy-start.3
  4.0 0.1 copy.17
  4.2 0.0 copy-done.5
  4.3 0.8 copy-done
  5.1 0.2 copy-done.1
  5.2 0.0 copy-done.2
  5.2 0.0 copy-done.3
  5.2 138.4 %shard_map.82 = bf16[4,16,3584]{2,1,0:T(8,128)(2,1)S(1)} custom-call(s32[8]{0:T(128)S(1)} %copy-done.2, s32[8]{0:T(128)S(1)} %copy-done.3, bf16[4,288,512]{2,1,0:T(8,128)(2,1)S(1)} %pad_maximum_fusion.cache_ref, bf16[4,4,64,128]{3,2,1,0:T(8,128)(2,1)S(1)} %slice.16.query_ref, bf16[4,256,64]{2,1,0:T(8,128)(2,1)S(1)} %bitcast.20, ...), custom_call_target="tpu_custom_call" | custom-call | flops 4294967296 | bytes 1179648 | tf_op jit(solution)/shard_map/pallas_call | solution.py:375
  143.6 0.4 copy.19
  144.0 1.1 reshape.35
  (3 shorter events, 0.1 us)
Async XLA Ops:
  1.2 1.2 slice-start
  3.0 1.0 copy-start.4
  3.1 1.2 copy-start.5
  4.0 1.1 copy-start
  4.0 1.2 copy-start.1
  4.0 1.2 copy-start.2
  4.0 1.2 copy-start.3

commit v4 on v3

--- a/solution.py
+++ b/solution.py
@@ -22,7 +22,7 @@
     scores = (dot_nt(absorbed, keys) + dot_nt(rotary, rope)) * scale
     scores = jnp.where(mask, scores, LOW)
     new_top = jnp.maximum(top, jnp.max(scores, axis=1, keepdims=True))
-    weights = jnp.where(mask, jnp.exp(scores - new_top), 0.0)
+    weights = jnp.exp(scores - new_top)
     rescale = jnp.exp(top - new_top)
     total = total * rescale + jnp.sum(weights, axis=1, keepdims=True)
     acc = acc * rescale + jnp.dot(weights.astype(BF16), keys, preferred_element_type=F32)
@@ -51,7 +51,8 @@
     latent, rope_width = up_ref.shape[2], rotary_ref.shape[2]
     width = value_ref.shape[2]
     groups = latent // rope_width
-    span = cache_ref.shape[1] * groups // (groups + 1)
+    span = cache_ref.shape[1]
+    share = span // groups
     rows = heads * tokens
     half = lax.axis_size("head") // 2
     me = lax.axis_index("head")
@@ -60,6 +61,12 @@
     group = lax.axis_index("req")
     not_first, not_last = mine > 0, mine < half - 1
 
+    for slot in range(slots):
+        both[group, slot, :span] = cache_ref[slot, :, :latent]
+        both[group, slot, span:] = jnp.concatenate(
+            [cache_ref[slot, g * share:(g + 1) * share, latent:] for g in range(groups)], axis=1
+        )
+
     barrier = pltpu.get_barrier_semaphore()
     pl.semaphore_signal(barrier, inc=1, device_id={"req": 1 - group}, device_id_type=MESH)
     pl.semaphore_signal(barrier, inc=1, device_id={"head": partner}, device_id_type=MESH)
@@ -71,13 +78,13 @@
 
     def swap():
         return pltpu.make_async_remote_copy(
-            src_ref=cache_ref, dst_ref=both.at[group], send_sem=swap_send, recv_sem=swap_recv,
+            src_ref=both.at[group], dst_ref=both.at[group], send_sem=swap_send, recv_sem=swap_recv,
             device_id={"req": 1 - group}, device_id_type=MESH,
         )
 
     def swap_in():
         return pltpu.make_async_remote_copy(
-            src_ref=cache_ref, dst_ref=both.at[1 - group], send_sem=swap_send, recv_sem=swap_recv,
+            src_ref=both.at[group], dst_ref=both.at[1 - group], send_sem=swap_send, recv_sem=swap_recv,
             device_id={"req": 1 - group}, device_id_type=MESH,
         )
 
@@ -174,7 +181,6 @@
 
     swap().start()
     load_weight().start()
-    both[group] = cache_ref[...]
 
     @pl.loop(0, slots)
     def _(slot):
@@ -205,7 +211,8 @@
     def merge(slot):
         send_partial(slot).wait_recv()
         send_stats(slot).wait_recv()
-        other_top, other_total = stats_in[slot, :, :1], stats_in[slot, :, 64:65]
+        other = jnp.transpose(stats_in[slot])
+        other_top, other_total = other[:, :1], other[:, 1:2]
         top = jnp.maximum(kept_top[slot], other_top)
         here = jnp.exp(kept_top[slot] - top)
         there = jnp.exp(other_top - top) * other_total
@@ -243,7 +250,7 @@
         query = full[slot].reshape(2 * rows, full.shape[3])
         own = own_ref[slot]
         zero = (
-            jnp.full((2 * rows, 1), LOW, F32),
+            jnp.full((2 * rows, 1), 0.5 * LOW, F32),
             jnp.zeros((2 * rows, 1), F32),
             jnp.zeros((2 * rows, latent), F32),
         )
@@ -296,7 +303,7 @@
         total = total_ref[rows:]
         partial[slot] = (acc_ref[rows:] / jnp.where(total > 0.0, total, 1.0)).astype(BF16)
         lane = lax.broadcasted_iota(jnp.int32, (rows, 128), 1)
-        stats[slot] = jnp.where(lane < 64, top_ref[rows:], total)
+        stats[slot] = jnp.transpose(jnp.where(lane % 2 == 0, top_ref[rows:], total))[:8]
         send_partial(slot).start()
         send_stats(slot).start()
         kept[slot] = acc_ref[:rows]
@@ -365,9 +372,6 @@
     query_rows = jnp.transpose(query_rows, (0, 1, 3, 2, 4, 5)).reshape(slots, heads, tokens, query_width)
     rotary_rows = query_rows[..., nope:].reshape(slots, rows, rope)
     own_rows = jnp.transpose(new_latent, (1, 0, 2, 3)).reshape(slots, tokens, cache_width)
-    packed = latent_cache[..., latent:].reshape(slots, packs, span // packs, rope)
-    packed = jnp.transpose(packed, (0, 2, 1, 3)).reshape(slots, span // packs, latent)
-    cache_rows = jnp.concatenate([latent_cache[..., :latent], packed], axis=1)
     deep = span + span // packs
     vmem, smem = pl.BlockSpec(memory_space=pltpu.VMEM), pl.BlockSpec(memory_space=pltpu.SMEM)
     padded = -(-cache_width // 128) * 128
@@ -389,8 +393,8 @@
             pltpu.VMEM((slots, rows, 1), F32),
             pltpu.VMEM((slots, rows, latent), BF16),
             pltpu.VMEM((slots, rows, latent), BF16),
-            pltpu.VMEM((slots, rows, 128), F32),
-            pltpu.VMEM((slots, rows, 128), F32),
+            pltpu.VMEM((slots, 8, rows), F32),
+            pltpu.VMEM((slots, 8, rows), F32),
             dma, dma, dma((slots,)), dma((slots,)),
             dma((slots, half - 1)), dma((slots, half - 1)), dma((slots, half - 1)), dma((slots, half - 1)),
             dma((slots,)), dma((slots,)), dma((slots,)), dma((slots,)),
@@ -412,7 +416,7 @@
             bytes_accessed=2 * slots * deep * latent,
             transcendentals=slots * rows * stripes * span,
         ),
-    )(slot_request, lengths, cache_rows, query_rows[..., :nope], rotary_rows, own_rows, key_up, value_up,
+    )(slot_request, lengths, latent_cache, query_rows[..., :nope], rotary_rows, own_rows, key_up, value_up,
       output_weight.reshape(depth, out_width))
     summed = jnp.transpose(summed.reshape(slots, pieces, per, reach), (2, 0, 1, 3))
     return summed.reshape(per, slots, out_width)

time: 145 us -> 140 us (0.966)
  Pallas kernels: 138 us -> 134 us
    pallas_call x1, Pallas kernels: 138 us -> 134 us  [shards(): pl.pallas_call(functools.partial(attention_kernel, scale, steps, cont), o...]
    slice x3 -> x0, local copies, waits for them, and re-layouts: 1.92 us -> none  [the longest x2 1.01 us: shards(): cache_rows = jnp.concatenate([latent_cache[..., :latent], packed], axis=1)]
where the time goes in v4:
time: 140 us
  Pallas kernels  134 us (96%)
  local copies, waits for them, and re-layouts  5.42 us (4%)
    pallas_call x1, Pallas kernels, shards(): pl.pallas_call(functools.partial(attention_kernel, scale, steps, cont), o...  134 us

profile of v4, /device:TPU:0, one launch (start us, length us, event | category | flops | bytes accessed | tf_op | source)
XLA Modules:
  0.0 139.8 jit_solution(17154103913469271247)
XLA Ops:
  0.0 1.0 copy.10
  1.0 1.1 copy.9
  2.3 0.0 copy-start
  2.3 0.0 copy-start.1
  2.3 0.0 copy-start.2
  2.3 0.0 copy-start.3
  2.3 1.8 %copy.11.cache_ref = bf16[4,256,576]{2,1,0:T(8,128)(2,1)S(1)} copy(bf16[4,256,576]{1,2,0:T(8,128)(2,1)} %param.8) | data formatting | bytes 2359296 | tf_op args[0]
  4.1 0.0 copy-done
  4.1 0.0 copy-done.1
  4.1 0.0 copy-done.2
  4.1 0.0 copy-done.3
  4.1 134.3 %shard_map.82 = bf16[4,16,3584]{2,1,0:T(8,128)(2,1)S(1)} custom-call(s32[8]{0:T(128)S(1)} %copy-done.2, s32[8]{0:T(128)S(1)} %copy-done.3, bf16[4,256,576]{2,1,0:T(8,128)(2,1)S(1)} %copy.11.cache_ref, bf16[4,4,64,128]{3,2,1,0:T(8,128)(2,1)S(1)} %slice.8.query_ref, bf16[4,256,64]{2,1,0:T(8,128)(2,1)S(1)} %bitcast.15, bf16[4,64,576]{2,1,0:T(8,128)(2,1)S(1)} %bitcast.14, ...), custom_call_target="tpu_custom_call" | custom-call | flops 4294967296 | bytes 1179648 | tf_op jit(solution)/shard_map/pallas_call | solution.py:379
  138.4 0.4 copy.12
  138.7 1.1 reshape.27
  (2 shorter events, 0.1 us)
Async XLA Ops:
  2.3 1.8 %copy-start = (bf16[4,128,512]{2,1,0:T(8,128)(2,1)S(1)}, bf16[4,128,512]{2,1,0:T(8,128)(2,1)}, u32[]{:S(2)}) copy-start(bf16[4,128,512]{2,1,0:T(8,128)(2,1)} %up_ref.1) | copy-start | bytes 1572868
  2.3 1.8 %copy-start.1 = (bf16[4,512,128]{2,1,0:T(8,128)(2,1)S(1)}, bf16[4,512,128]{2,1,0:T(8,128)(2,1)}, u32[]{:S(2)}) copy-start(bf16[4,512,128]{2,1,0:T(8,128)(2,1)} %value_ref.1) | copy-start | bytes 1572868
  2.3 1.8 %copy-start.2 = (s32[8]{0:T(128)S(1)}, s32[8]{0:T(128)}, u32[]{:S(2)}) copy-start(s32[8]{0:T(128)} %request_ref.1) | copy-start | bytes 100
  2.3 1.8 %copy-start.3 = (s32[8]{0:T(128)S(1)}, s32[8]{0:T(128)}, u32[]{:S(2)}) copy-start(s32[8]{0:T(128)} %length_ref.1) | copy-start | bytes 100

commit v5 on v4

--- a/solution.py
+++ b/solution.py
@@ -364,7 +364,7 @@
     pieces = max(1, 16 // per)
     depth, out_width = heads * vhead, output_weight.shape[2]
     reach = out_width // pieces
-    chunk = 896 if reach % 896 == 0 else reach
+    chunk = 1792 if reach % 1792 == 0 else reach
     chunks = reach // chunk
     rope = cache_width - latent
     packs = latent // rope

time: 140 us -> 139 us (level)
    pallas_call x1, Pallas kernels: 134 us -> 133 us  [shards(): pl.pallas_call(functools.partial(attention_kernel, scale, steps, cont), o...]
where the time goes in v5:
time: 139 us; the launch traced here: 138 us
  Pallas kernels  133 us (96%)
  local copies, waits for them, and re-layouts  5.42 us (4%)
    pallas_call x1, Pallas kernels, shards(): pl.pallas_call(functools.partial(attention_kernel, scale, steps, cont), o...  133 us

profile of v5, /device:TPU:0, one launch (start us, length us, event | category | flops | bytes accessed | tf_op | source)
XLA Modules:
  0.0 138.3 jit_solution(10585815835998508700)
XLA Ops:
  0.0 1.0 copy.10
  1.0 1.1 copy.9
  2.3 0.0 copy-start
  2.3 0.0 copy-start.1
  2.3 0.0 copy-start.2
  2.3 0.0 copy-start.3
  2.3 1.8 %copy.11.cache_ref = bf16[4,256,576]{2,1,0:T(8,128)(2,1)S(1)} copy(bf16[4,256,576]{1,2,0:T(8,128)(2,1)} %param.8) | data formatting | bytes 2359296 | tf_op args[0]
  4.1 0.0 copy-done
  4.1 0.0 copy-done.1
  4.1 0.0 copy-done.2
  4.1 0.0 copy-done.3
  4.1 132.7 %shard_map.82 = bf16[4,16,3584]{2,1,0:T(8,128)(2,1)S(1)} custom-call(s32[8]{0:T(128)S(1)} %copy-done.2, s32[8]{0:T(128)S(1)} %copy-done.3, bf16[4,256,576]{2,1,0:T(8,128)(2,1)S(1)} %copy.11.cache_ref, bf16[4,4,64,128]{3,2,1,0:T(8,128)(2,1)S(1)} %slice.8.query_ref, bf16[4,256,64]{2,1,0:T(8,128)(2,1)S(1)} %bitcast.15, bf16[4,64,576]{2,1,0:T(8,128)(2,1)S(1)} %bitcast.14, ...), custom_call_target="tpu_custom_call" | custom-call | flops 4294967296 | bytes 1179648 | tf_op jit(solution)/shard_map/pallas_call | solution.py:379
  136.9 0.4 copy.12
  137.2 1.1 reshape.27
  (2 shorter events, 0.1 us)
Async XLA Ops:
  2.3 1.8 %copy-start = (bf16[4,128,512]{2,1,0:T(8,128)(2,1)S(1)}, bf16[4,128,512]{2,1,0:T(8,128)(2,1)}, u32[]{:S(2)}) copy-start(bf16[4,128,512]{2,1,0:T(8,128)(2,1)} %up_ref.1) | copy-start | bytes 1572868
  2.3 1.8 %copy-start.1 = (bf16[4,512,128]{2,1,0:T(8,128)(2,1)S(1)}, bf16[4,512,128]{2,1,0:T(8,128)(2,1)}, u32[]{:S(2)}) copy-start(bf16[4,512,128]{2,1,0:T(8,128)(2,1)} %value_ref.1) | copy-start | bytes 1572868
  2.3 1.8 %copy-start.2 = (s32[8]{0:T(128)S(1)}, s32[8]{0:T(128)}, u32[]{:S(2)}) copy-start(s32[8]{0:T(128)} %request_ref.1) | copy-start | bytes 100
  2.3 1.8 %copy-start.3 = (s32[8]{0:T(128)S(1)}, s32[8]{0:T(128)}, u32[]{:S(2)}) copy-start(s32[8]{0:T(128)} %length_ref.1) | copy-start | bytes 100
